TPU v7x, 32 devices: a whole 2x2x4 slice. The times are simulated.
32 devices in a mesh: st: 4 (over y, core), col: 8 (over z, x).
Axes of the slice: x: 2, y: 2, z: 4, core: 2. Of those that a mesh axis runs over, the one named last changes fastest.
Arguments:
- forcing: bfloat16 [8, 2048, 2048], P('st', None, 'col'), may hold values from -6 to 6
- operator_rows: bfloat16 [8, 2048, 2048], P('st', 'col'), may hold values from -0.078125 to 0.078125
- counts: int32 [8], P('st'), may hold values from 1 to 3, as said below
- owner_map: int32 [8, 8], P('st'), may hold values from 0 to 7, each once within a row
Outputs:
- adjoint: bfloat16 [8, 2048, 2048], P('st', None, 'col')
Inputs may be any that keep to these rules, and one draw needn't show every extreme that they name: `counts`: some station has exactly 3 terms. `owner_map`: each station's row is a permutation of the row blocks.
All inputs are finite; a program needn't handle non-finite values.
Results may differ from a plain program's by a relative error of at most 0.015.
Values may be sent and summed in bfloat16 or wider, within the bound.
A program may use at most 128 MiB of HBM per device.

v0:
```python
import functools

import jax
import jax.numpy as jnp
from jax import lax
from jax.experimental import pallas as pl
from jax.experimental.pallas import tpu as pltpu
from jax.sharding import PartitionSpec as P

MESH = pl.DeviceIdType.MESH
TERMS = 3


def ring_index(pos, n):
    if n % 2:
        return pos
    return jnp.where(pos < n // 2, 2 * pos, 2 * (n - 1 - pos) + 1)


def ring_position(index, n):
    if n % 2:
        return index
    return jnp.where(index % 2 == 0, index // 2, n - 1 - index // 2)


def kernel(n, sections, counts_ref, slots_ref, rows_ref, force_ref, out_ref, matrix, phi, stage, total, incoming,
           local_sem, send_sem, recv_sem, turn_sem, state_send, state_recv):
    stations, block, size = rows_ref.shape
    half = block // 2
    me, place = lax.axis_index("col"), lax.axis_index("st")
    pos = ring_position(me, n)
    peers = (ring_index((pos + 1) % n, n), ring_index((pos + n - 1) % n, n))
    top = sections - 1

    barrier = pltpu.get_barrier_semaphore()
    for peer in peers:
        pl.semaphore_signal(barrier, inc=1, device_id={"col": peer}, device_id_type=MESH)

    @pl.when(place > 0)
    def _():
        pl.semaphore_signal(barrier, inc=1, device_id={"st": place - 1}, device_id_type=MESH)

    @pl.when(place < top)
    def _():
        pl.semaphore_signal(barrier, inc=1, device_id={"st": place + 1}, device_id_type=MESH)

    pl.semaphore_wait(barrier, 2 + jnp.where(place > 0, 1, 0) + jnp.where(place < top, 1, 0))

    own = [pltpu.make_async_copy(rows_ref.at[j], matrix.at[j, me], local_sem.at[j]) for j in range(stations)]
    for copy in own:
        copy.start()

    if sections > 1:
        @pl.when(place == top - 1)
        def _():
            pl.semaphore_wait(turn_sem, 1)

    def copy_of(j, d, t):
        slot = ring_index((pos - t + n) % n if d == 0 else (pos + t) % n, n)
        part = pl.ds(d * half, half)
        return pltpu.make_async_remote_copy(
            src_ref=rows_ref.at[j, part] if t == 0 else matrix.at[j, slot, part],
            dst_ref=matrix.at[j, slot, part],
            send_sem=send_sem.at[j, d, t],
            recv_sem=recv_sem.at[j, d, t],
            device_id={"col": peers[d]},
            device_id_type=MESH,
        )

    order = list(reversed(range(stations)))
    flows = [(j, d) for j in order for d in range(2)]
    copies = {}
    for t in range(n - 1):
        for j, d in flows:
            if t > 0:
                copies[j, d, t - 1].wait_recv()
            copies[j, d, t] = copy_of(j, d, t)
            copies[j, d, t].start()

    if sections > 1:
        @pl.when(place == top)
        def _():
            pl.semaphore_signal(turn_sem, inc=1, device_id={"st": place - 1}, device_id_type=MESH)

    for j, d in flows:
        copies[j, d, n - 2].wait_recv()
    for copy in copies.values():
        copy.wait_send()
    for copy in own:
        copy.wait()

    handoff = pltpu.make_async_remote_copy(
        src_ref=out_ref.at[order[-1]],
        dst_ref=incoming,
        send_sem=state_send,
        recv_sem=state_recv,
        device_id={"st": jnp.maximum(place - 1, 0)},
        device_id_type=MESH,
    )

    @pl.when(place == top)
    def _():
        incoming[...] = jnp.zeros_like(incoming)

    @pl.when(place < top)
    def _():
        handoff.wait_recv()

    group = max(1, min(n, 512 // block))
    while n % group:
        group -= 1
    for j in order:
        before = incoming if j == order[0] else out_ref.at[j + 1]

        def begin(b, _):
            at = pl.ds(pl.multiple_of(b * block, block), block)
            start = (before[at, :].astype(jnp.float32) + force_ref[j, at, :].astype(jnp.float32)).astype(jnp.bfloat16)
            phi[at, :] = start
            total[at, :] = start.astype(jnp.float32)
            return 0

        lax.fori_loop(0, n, begin, 0)

        def power(k, _):
            def product(i, _):
                at = pl.ds(i * group, group)
                rows = matrix[j, at].reshape(group * block, size)
                made = jnp.dot(rows, phi[...], preferred_element_type=jnp.float32).astype(jnp.bfloat16)
                stage[at] = made.reshape(group, block, made.shape[1])
                return 0

            lax.fori_loop(0, n // group, product, 0)
            counted = jnp.full((block, phi.shape[1]), counts_ref[j], jnp.int32) > k

            def settle(b, _):
                at = pl.ds(pl.multiple_of(b * block, block), block)
                piece = stage[slots_ref[j, b]]
                phi[at, :] = piece
                total[at, :] += jnp.where(counted, piece.astype(jnp.float32), 0.0)
                return 0

            lax.fori_loop(0, n, settle, 0)
            return 0

        lax.fori_loop(0, TERMS, power, 0)
        out_ref[j] = (0.7 * total[...]).astype(jnp.bfloat16)

    @pl.when(place > 0)
    def _():
        handoff.start()
        handoff.wait_send()


def shards(forcing, operator_rows, counts, owner_map):
    n = lax.axis_size("col")
    sections = lax.axis_size("st")
    ids = jnp.arange(n, dtype=jnp.int32)
    slots = jnp.sum(jnp.where(owner_map[:, None, :] == ids[None, :, None], ids[None, None, :], 0), axis=2).astype(jnp.int32)
    stations, block, size = operator_rows.shape
    width = forcing.shape[2]
    vmem = pl.BlockSpec(memory_space=pltpu.VMEM)
    smem = pl.BlockSpec(memory_space=pltpu.SMEM)
    return pl.pallas_call(
        functools.partial(kernel, n, sections),
        out_shape=jax.ShapeDtypeStruct(forcing.shape, forcing.dtype),
        in_specs=[smem, smem, pl.BlockSpec(memory_space=pl.ANY), vmem],
        out_specs=vmem,
        scratch_shapes=[
            pltpu.VMEM((stations, n, block, size), jnp.bfloat16),
            pltpu.VMEM((size, width), jnp.bfloat16),
            pltpu.VMEM((n, block, width), jnp.bfloat16),
            pltpu.VMEM((size, width), jnp.float32),
            pltpu.VMEM((size, width), jnp.bfloat16),
            pltpu.SemaphoreType.DMA((stations,)),
            pltpu.SemaphoreType.DMA((stations, 2, n - 1)),
            pltpu.SemaphoreType.DMA((stations, 2, n - 1)),
            pltpu.SemaphoreType.REGULAR,
            pltpu.SemaphoreType.DMA,
            pltpu.SemaphoreType.DMA,
        ],
        compiler_params=pltpu.CompilerParams(collective_id=0, has_side_effects=True, vmem_limit_bytes=48 * 1024 * 1024),
        name="gather_and_march",
    )(counts, slots, operator_rows, forcing)


def solution(mesh):
    in_specs = (P("st", None, "col"), P("st", "col", None), P("st"), P("st", None))
    out_specs = P("st", None, "col")
    return jax.shard_map(shards, mesh=mesh, in_specs=in_specs, out_specs=out_specs, check_vma=False)
```

profile of v0, /device:TPU:0, one launch (start us, length us, event | category | flops | bytes accessed | tf_op | source)
XLA Modules:
  0.0 245.3 jit_solution(12961840945839283571)
XLA Ops:
  0.0 0.8 select_reduce_fusion.slots_ref
  0.8 0.0 copy-start
  0.8 1.6 copy-done
  2.4 0.0 copy-start.1
  2.4 0.7 copy-done.1
  3.1 240.9 %gather_and_march.1 = bf16[2,2048,256]{2,1,0:T(8,128)(2,1)S(1)} custom-call(s32[2]{0:T(128)S(1)} %copy-done.1, s32[2,8]{1,0:T(2,128)S(1)} %select_reduce_fusion.slots_ref, bf16[2,256,2048]{2,1,0:T(8,128)(2,1)S(1)} %copy-done, bf16[2,2048,256]{2,1,0:T(8,128)(2,1)} %force_ref.1), custom_call_target="tpu_custom_call" | custom-call | tf_op jit(solution)/shard_map/gather_and_march/pallas_call | solution.py:163
  244.0 1.3 copy.6
Async XLA Ops:
  0.8 1.6 copy-start
  2.4 0.7 copy-start.1
where the time goes:
time: 245 us
  Pallas kernels  241 us (98%)
  local copies, waits for them, and re-layouts  3.57 us (1%)
    pallas_call x1, Pallas kernels, shards(): pl.pallas_call(functools.partial(kernel, n, sections), out_shape=jax.Shap...  241 us

commit v1 on v0

--- a/solution.py
+++ b/solution.py
@@ -9,6 +9,7 @@
 
 MESH = pl.DeviceIdType.MESH
 TERMS = 3
+PIECES = 1
 
 
 def ring_index(pos, n):
@@ -23,7 +24,7 @@
     return jnp.where(index % 2 == 0, index // 2, n - 1 - index // 2)
 
 
-def kernel(n, sections, counts_ref, slots_ref, rows_ref, force_ref, out_ref, matrix, phi, stage, total, incoming,
+def kernel(n, sections, counts_ref, slots_ref, rows_ref, force_ref, out_ref, matrix, phis, incoming,
            local_sem, send_sem, recv_sem, turn_sem, state_send, state_recv):
     stations, block, size = rows_ref.shape
     half = block // 2
@@ -89,66 +90,62 @@
     for copy in own:
         copy.wait()
 
-    handoff = pltpu.make_async_remote_copy(
-        src_ref=out_ref.at[order[-1]],
-        dst_ref=incoming,
-        send_sem=state_send,
-        recv_sem=state_recv,
-        device_id={"st": jnp.maximum(place - 1, 0)},
-        device_id_type=MESH,
-    )
+    pieces = PIECES if size % (PIECES * 16) == 0 and n % PIECES == 0 else 1
+    span = size // pieces
+
+    def handoff(i):
+        return pltpu.make_async_remote_copy(
+            src_ref=out_ref.at[order[-1], pl.ds(i * span, span)],
+            dst_ref=incoming.at[pl.ds(i * span, span)],
+            send_sem=state_send.at[i],
+            recv_sem=state_recv.at[i],
+            device_id={"st": jnp.maximum(place - 1, 0)},
+            device_id_type=MESH,
+        )
 
     @pl.when(place == top)
     def _():
         incoming[...] = jnp.zeros_like(incoming)
 
-    @pl.when(place < top)
-    def _():
-        handoff.wait_recv()
+    def product(j, source, first, count):
+        rows = jnp.concatenate([matrix[j, slots_ref[j, first + b]] for b in range(count)], axis=0)
+        return jnp.dot(rows, source, preferred_element_type=jnp.float32).astype(jnp.bfloat16)
 
-    group = max(1, min(n, 512 // block))
-    while n % group:
-        group -= 1
     for j in order:
-        before = incoming if j == order[0] else out_ref.at[j + 1]
+        for i in range(pieces):
+            at = pl.ds(i * span, span)
+            if j == order[0]:
+                @pl.when(place < top)
+                def _():
+                    handoff(i).wait_recv()
+                before = incoming[at, :]
+            else:
+                before = out_ref[j + 1, at, :]
+            phis[0, at, :] = (before.astype(jnp.float32) + force_ref[j, at, :].astype(jnp.float32)).astype(jnp.bfloat16)
 
-        def begin(b, _):
-            at = pl.ds(pl.multiple_of(b * block, block), block)
-            start = (before[at, :].astype(jnp.float32) + force_ref[j, at, :].astype(jnp.float32)).astype(jnp.bfloat16)
-            phi[at, :] = start
-            total[at, :] = start.astype(jnp.float32)
+        def power(k, _):
+            phis[k + 1] = product(j, phis[k], 0, n)
             return 0
 
-        lax.fori_loop(0, n, begin, 0)
-
-        def power(k, _):
-            def product(i, _):
-                at = pl.ds(i * group, group)
-                rows = matrix[j, at].reshape(group * block, size)
-                made = jnp.dot(rows, phi[...], preferred_element_type=jnp.float32).astype(jnp.bfloat16)
-                stage[at] = made.reshape(group, block, made.shape[1])
-                return 0
-
-            lax.fori_loop(0, n // group, product, 0)
-            counted = jnp.full((block, phi.shape[1]), counts_ref[j], jnp.int32) > k
-
-            def settle(b, _):
-                at = pl.ds(pl.multiple_of(b * block, block), block)
-                piece = stage[slots_ref[j, b]]
-                phi[at, :] = piece
-                total[at, :] += jnp.where(counted, piece.astype(jnp.float32), 0.0)
-                return 0
-
-            lax.fori_loop(0, n, settle, 0)
-            return 0
-
-        lax.fori_loop(0, TERMS, power, 0)
-        out_ref[j] = (0.7 * total[...]).astype(jnp.bfloat16)
+        lax.fori_loop(0, TERMS - 1, power, 0)
+        for i in range(pieces):
+            at = pl.ds(i * span, span)
+            terms = [phis[k, at, :] for k in range(TERMS)]
+            terms.append(product(j, phis[TERMS - 1], i * (n // pieces), n // pieces))
+            total = terms[0].astype(jnp.float32)
+            for k in range(1, TERMS + 1):
+                counted = jnp.full(total.shape, counts_ref[j], jnp.int32) >= k
+                total += jnp.where(counted, terms[k].astype(jnp.float32), 0.0)
+            out_ref[j, at, :] = (0.7 * total).astype(jnp.bfloat16)
+            if j == order[-1]:
+                @pl.when(place > 0)
+                def _():
+                    handoff(i).start()
 
     @pl.when(place > 0)
     def _():
-        handoff.start()
-        handoff.wait_send()
+        for i in range(pieces):
+            handoff(i).wait_send()
 
 
 def shards(forcing, operator_rows, counts, owner_map):
@@ -167,16 +164,14 @@
         out_specs=vmem,
         scratch_shapes=[
             pltpu.VMEM((stations, n, block, size), jnp.bfloat16),
-            pltpu.VMEM((size, width), jnp.bfloat16),
-            pltpu.VMEM((n, block, width), jnp.bfloat16),
-            pltpu.VMEM((size, width), jnp.float32),
+            pltpu.VMEM((TERMS, size, width), jnp.bfloat16),
             pltpu.VMEM((size, width), jnp.bfloat16),
             pltpu.SemaphoreType.DMA((stations,)),
             pltpu.SemaphoreType.DMA((stations, 2, n - 1)),
             pltpu.SemaphoreType.DMA((stations, 2, n - 1)),
             pltpu.SemaphoreType.REGULAR,
-            pltpu.SemaphoreType.DMA,
-            pltpu.SemaphoreType.DMA,
+            pltpu.SemaphoreType.DMA((PIECES,)),
+            pltpu.SemaphoreType.DMA((PIECES,)),
         ],
         compiler_params=pltpu.CompilerParams(collective_id=0, has_side_effects=True, vmem_limit_bytes=48 * 1024 * 1024),
         name="gather_and_march",

time: 245 us -> 233 us (0.951)
  Pallas kernels: 241 us -> 228 us
    pallas_call x1, Pallas kernels: 241 us -> 228 us  [shards(): pl.pallas_call(functools.partial(kernel, n, sections), out_shape=jax.Shap...]
where the time goes in v1:
time: 233 us; the launch traced here: 232 us
  Pallas kernels  228 us (98%)
  local copies, waits for them, and re-layouts  3.57 us (2%)
    pallas_call x1, Pallas kernels, shards(): pl.pallas_call(functools.partial(kernel, n, sections), out_shape=jax.Shap...  228 us

profile of v1, /device:TPU:0, one launch (start us, length us, event | category | flops | bytes accessed | tf_op | source)
XLA Modules:
  0.0 232.5 jit_solution(7995936732182880170)
XLA Ops:
  0.0 0.8 select_reduce_fusion.slots_ref
  0.8 0.0 copy-start
  0.8 1.6 copy-done
  2.4 0.0 copy-start.1
  2.4 0.7 copy-done.1
  3.1 228.1 %gather_and_march.1 = bf16[2,2048,256]{2,1,0:T(8,128)(2,1)S(1)} custom-call(s32[2]{0:T(128)S(1)} %copy-done.1, s32[2,8]{1,0:T(2,128)S(1)} %select_reduce_fusion.slots_ref, bf16[2,256,2048]{2,1,0:T(8,128)(2,1)S(1)} %copy-done, bf16[2,2048,256]{2,1,0:T(8,128)(2,1)} %force_ref.1), custom_call_target="tpu_custom_call" | custom-call | tf_op jit(solution)/shard_map/gather_and_march/pallas_call | solution.py:160
  231.1 1.3 copy.6
Async XLA Ops:
  0.8 1.6 copy-start
  2.4 0.7 copy-start.1
